TPU v7x, 32 devices: a whole 2x2x4 slice. The times are simulated.
32 devices in a mesh: groups: 2 (over y), sector: 4 (over z), chan: 2 (over x), rep: 2 (over core).
Axes of the slice: x: 2, y: 2, z: 4, core: 2. Of those that a mesh axis runs over, the one named last changes fastest.
Arguments:
- theta: bfloat16 [48, 256, 256], P(('groups', 'sector')), parts along dimension 0, may hold values from -6 to 6
- left_env: bfloat16 [12, 24, 256, 256], P(('groups', 'chan'), 'sector', 'rep'), parts along dimension 0, may hold values from -0.375 to 0.375
- right_env: bfloat16 [12, 24, 256, 256], P(('groups', 'chan'), 'sector'), parts along dimension 0, may hold values from -0.375 to 0.375
- coef: float32 [48, 6, 4], P(('groups', 'sector'), 'chan'), parts along dimension 0, may hold values from -0.6 to 0.6
- term_slot: int32 [48, 6, 4], P(('groups', 'sector'), 'chan'), parts along dimension 0, may hold values from 0 to 7, as said below
- need: int32 [8, 4, 2], P('groups'), parts along dimension 0, may hold values from 0 to 5
- dims: int32 [48, 2], P(('groups', 'sector')), parts along dimension 0, may hold values from 64 to 256
Outputs:
- product: float32 [48, 256, 256], P(('groups', 'sector'), 'rep'), parts along dimension 0
There are 2 independent parts, one for each index of `groups`. A program takes and returns all parts, laid end to end along the dimension named above; each array names one. Nothing has to cross between parts.
Inputs may be any that keep to these rules, and one draw needn't show every extreme that they name: `term_slot`: for each owner of 6 blocks and each shard of 3 channels, every slot 0 to 4 * 2 - 1 is named by at least one term.
All inputs are finite; a program needn't handle non-finite values.
Results may differ from a plain program's by a relative error of at most 0.0029.
Values may be sent and summed in bfloat16 or wider, within the bound.
A program may use at most 64 MiB of HBM per device.

v0:
```python
import jax
import jax.numpy as jnp
from jax import lax
from jax.sharding import PartitionSpec as P


def live_mask(counts, order_rows, order_cols, row_start):
    row_index = row_start + jnp.arange(order_rows, dtype=jnp.int32)
    col_index = jnp.arange(order_cols, dtype=jnp.int32)
    return (row_index[None, :, None] < counts[:, 0][:, None, None]) & (
        col_index[None, None, :] < counts[:, 1][:, None, None]
    )


def body(theta, left_env, right_env, coef, term_slot, need, dims):
    blocks = theta.shape[0]
    order = theta.shape[2]
    half_rows = left_env.shape[2]
    owner = lax.axis_index("sector")
    masked = jnp.where(live_mask(dims, order, order, 0), theta, jnp.zeros_like(theta))
    outgoing = jnp.take(masked, jnp.take(need, owner, axis=1), axis=0)
    received = lax.all_to_all(outgoing, "sector", split_axis=0, concat_axis=0, tiled=True)
    received = received.reshape(-1, order, order)
    total = jnp.zeros((blocks, half_rows, order), jnp.float32)
    for position in range(term_slot.shape[2]):
        source = jnp.take(received, term_slot[:, :, position], axis=0)
        partial_left = jnp.einsum(
            "wohm,owmn->owhn", left_env, source, preferred_element_type=jnp.float32
        ).astype(jnp.bfloat16)
        image = jnp.einsum(
            "owhn,wopn->owhp", partial_left, right_env, preferred_element_type=jnp.float32
        )
        total = total + jnp.sum(image * coef[:, :, position][:, :, None, None], axis=1)
    summed = lax.psum(total, "chan")
    start_row = lax.axis_index("rep") * half_rows
    return jnp.where(live_mask(dims, half_rows, order, start_row), summed, jnp.zeros_like(summed))


def solution(mesh):
    in_specs = (
        P(("groups", "sector"), None, None),
        P(("groups", "chan"), "sector", "rep", None),
        P(("groups", "chan"), "sector", None, None),
        P(("groups", "sector"), "chan", None),
        P(("groups", "sector"), "chan", None),
        P("groups", None, None),
        P(("groups", "sector"), None),
    )
    out_specs = P(("groups", "sector"), "rep", None)
    return jax.shard_map(body, mesh=mesh, in_specs=in_specs, out_specs=out_specs, check_vma=False)
```

profile of v0, /device:TPU:0, one launch (start us, length us, event | category | flops | bytes accessed | tf_op | source)
XLA Modules:
  0.0 117.5 jit_solution(5972954150123478547)
XLA Ops:
  6.5 0.0 copy-start
  6.5 0.9 dynamic-slice_select_fusion
  7.4 0.1 copy.29
  7.6 0.1 copy.32
  7.7 0.1 reshape.198
  7.8 0.8 slice_bitcast_fusion.1
  8.5 0.1 copy.30
  8.6 0.1 iota_compare_fusion
  8.7 1.5 %and_select_fusion = bf16[6,256,256]{2,1,0:T(8,128)(2,1)S(1)} fusion(bf16[6,256,256]{2,1,0:T(8,128)(2,1)} %param.9, pred[6,256]{1,0:T(8,128)(4,1)S(1)} %get-tuple-element.28, pred[6,256]{1,0:T(8,128)(4,1)S(1)} %get-tuple-element.27), kind=kLoop, calls=%fused_computation.21 | loop fusion | flops 786432 | bytes 1575936 | tf_op jit(solution)/shard_map/jit(_where)/select_n | solution.py:20
  10.2 1.6 %gather_fusion = bf16[8,256,256]{2,1,0:T(8,128)(2,1)} fusion(bf16[6,256,256]{2,1,0:T(8,128)(2,1)S(1)} %and_select_fusion, s32[1024]{0:T(1024)S(1)} %pad_clamp_fusion.4), kind=kCustom, calls=%fused_computation.4 | custom fusion | bytes 2097184 | tf_op jit(solution)/shard_map/jit(_take)/gather | solution.py:21
  11.8 0.0 copy-start.1
  11.8 0.0 copy-start.2
  11.8 2.4 %broadcast_select_fusion = bf16[4,2,256,256]{3,2,1,0:T(8,128)(2,1)} fusion(bf16[4,2,256,256]{3,2,1,0:T(8,128)(2,1)} %bitcast.40, pred[4,2]{1,0:T(4,128)(4,1)S(1)} %copy.30), kind=kLoop, calls=%fused_computation.34 | loop fusion | flops 524288 | bytes 2097160 | tf_op jit(solution)/shard_map/jit(_take)/select_n | solution.py:21
  14.2 6.3 %all-to-all-start = ((bf16[4,2,256,256]{3,2,1,0:T(8,128)(2,1)}), bf16[4,2,256,256]{3,2,1,0:T(8,128)(2,1)S(1)}, u32[]{:S(2)}, u32[]{:S(2)}) async-start(bf16[4,2,256,256]{3,2,1,0:T(8,128)(2,1)} %broadcast_select_fusion), calls=%async_computation | async-start | bytes 2097152 | tf_op jit(solution)/shard_map/all_to_all | solution.py:22
  20.5 0.0 all-reduce.2.cloned.1.call-start
  20.5 0.0 copy-done.1
  20.5 0.1 copy.41
  20.6 0.1 reshape.221
  20.7 0.1 copy.40
  20.8 0.0 copy-done.2
  20.9 0.1 copy.51
  21.0 0.1 copy.37
  21.1 0.1 reshape.217
  21.1 0.1 copy.36
  21.3 0.1 copy.50
  21.3 0.1 copy.33
  21.4 0.1 reshape.213
  21.5 0.1 copy.28
  21.6 0.1 copy.49
  21.7 0.1 copy.45
  21.8 0.1 reshape.225
  21.9 0.1 copy.44
  22.0 0.1 copy.52
  22.1 24.1 %all-to-all-done = bf16[4,2,256,256]{3,2,1,0:T(8,128)(2,1)S(1)} async-done(((bf16[4,2,256,256]{3,2,1,0:T(8,128)(2,1)}), bf16[4,2,256,256]{3,2,1,0:T(8,128)(2,1)S(1)}, u32[]{:S(2)}, u32[]{:S(2)}) %all-to-all-start) | async-done | bytes 1048608 | tf_op jit(solution)/shard_map/all_to_all | solution.py:22
  46.2 2.3 %gather_fusion.3 = bf16[18,256,256]{2,1,0:T(8,128)(2,1)} fusion(bf16[8,256,256]{2,1,0:T(8,128)(2,1)S(1)} %bitcast.36, s32[1024]{0:T(1024)S(1)} %pad_clamp_fusion.1), kind=kCustom, calls=%fused_computation.2.clone | custom fusion | bytes 4718664 | tf_op jit(solution)/shard_map/jit(_take)/gather | solution.py:26
  48.6 2.3 %gather_fusion.2 = bf16[18,256,256]{2,1,0:T(8,128)(2,1)} fusion(bf16[8,256,256]{2,1,0:T(8,128)(2,1)S(1)} %bitcast.37, s32[1024]{0:T(1024)S(1)} %pad_clamp_fusion.2), kind=kCustom, calls=%fused_computation.1.clone | custom fusion | bytes 4718664 | tf_op jit(solution)/shard_map/jit(_take)/gather | solution.py:26
  50.9 2.3 %gather_fusion.1 = bf16[18,256,256]{2,1,0:T(8,128)(2,1)} fusion(bf16[8,256,256]{2,1,0:T(8,128)(2,1)S(1)} %bitcast.38, s32[1024]{0:T(1024)S(1)} %pad_clamp_fusion.3), kind=kCustom, calls=%fused_computation.clone | custom fusion | bytes 4718664 | tf_op jit(solution)/shard_map/jit(_take)/gather | solution.py:26
  53.2 2.3 %gather_fusion.4 = bf16[18,256,256]{2,1,0:T(8,128)(2,1)} fusion(bf16[8,256,256]{2,1,0:T(8,128)(2,1)S(1)} %bitcast.39, s32[1024]{0:T(1024)S(1)} %pad_clamp_fusion), kind=kCustom, calls=%fused_computation.3.clone | custom fusion | bytes 4718664 | tf_op jit(solution)/shard_map/jit(_take)/gather | solution.py:26
  55.5 0.0 copy-done
  55.5 3.5 %multiply_reduce_fusion.1 = f32[6,128,256]{2,1,0:T(8,128)S(1)} fusion(bf16[3,6,256,256]{3,2,1,0:T(8,128)(2,1)S(1)} %copy-done, f32[6,3]{1,0:T(8,128)S(1)} %bitcast.45, bf16[6,3,256,256]{3,2,1,0:T(8,128)(2,1)} %bitcast.44, pred[6,3]{1,0:T(8,128)(4,1)S(1)} %copy.40, bf16[3,6,128,256]{3,2,1,0:T(8,128)(2,1)} %param.10), kind=kOutput, calls=%fused_computation.14 | convolution fusion | flops 606732288 | bytes 6684762 | tf_op jit(solution)/shard_map/owhn,wopn->owhp/dot_general | solution.py:30
  59.0 4.4 %multiply_reduce_fusion.2 = f32[6,128,256]{2,1,0:T(8,128)} fusion(bf16[3,6,256,256]{3,2,1,0:T(8,128)(2,1)S(1)} %copy-done, f32[6,3]{1,0:T(8,128)S(1)} %bitcast.46, bf16[6,3,256,256]{3,2,1,0:T(8,128)(2,1)} %bitcast.43, pred[6,3]{1,0:T(8,128)(4,1)S(1)} %copy.36, bf16[3,6,128,256]{3,2,1,0:T(8,128)(2,1)} %param.10), kind=kOutput, calls=%fused_computation.15 | convolution fusion | flops 606732288 | bytes 6684762 | tf_op jit(solution)/shard_map/owhn,wopn->owhp/dot_general | solution.py:30
  63.4 4.4 %multiply_reduce_fusion.3 = f32[6,128,256]{2,1,0:T(8,128)} fusion(bf16[3,6,256,256]{3,2,1,0:T(8,128)(2,1)S(1)} %copy-done, f32[6,3]{1,0:T(8,128)S(1)} %bitcast.47, bf16[6,3,256,256]{3,2,1,0:T(8,128)(2,1)} %bitcast.42, pred[6,3]{1,0:T(8,128)(4,1)S(1)} %copy.28, bf16[3,6,128,256]{3,2,1,0:T(8,128)(2,1)} %param.10), kind=kOutput, calls=%fused_computation.16 | convolution fusion | flops 606732288 | bytes 6684762 | tf_op jit(solution)/shard_map/owhn,wopn->owhp/dot_general | solution.py:30
  67.8 4.4 %multiply_reduce_fusion = f32[6,128,256]{2,1,0:T(8,128)} fusion(bf16[3,6,256,256]{3,2,1,0:T(8,128)(2,1)S(1)} %copy-done, f32[6,3]{1,0:T(8,128)S(1)} %bitcast.48, bf16[6,3,256,256]{3,2,1,0:T(8,128)(2,1)} %bitcast.41, pred[6,3]{1,0:T(8,128)(4,1)S(1)} %copy.44, bf16[3,6,128,256]{3,2,1,0:T(8,128)(2,1)} %param.10), kind=kOutput, calls=%fused_computation.13 | convolution fusion | flops 606732288 | bytes 6684762 | tf_op jit(solution)/shard_map/owhn,wopn->owhp/dot_general | solution.py:30
  72.2 2.7 %add_add_fusion = f32[6,128,256]{2,1,0:T(8,128)} fusion(f32[6,128,256]{2,1,0:T(8,128)} %multiply_reduce_fusion, f32[6,128,256]{2,1,0:T(8,128)S(1)} %multiply_reduce_fusion.1, f32[6,128,256]{2,1,0:T(8,128)} %multiply_reduce_fusion.3, f32[6,128,256]{2,1,0:T(8,128)} %multiply_reduce_fusion.2), kind=kLoop, calls=%fused_computation.35 | loop fusion | flops 589824 | bytes 3932160 | tf_op jit(solution)/shard_map/add | solution.py:33
  74.9 0.0 all-reduce.2.cloned.1.call-update
  74.9 0.1 broadcast_compare_fusion
  75.0 33.5 %all-reduce.2.cloned.1.call-done = f32[6,128,256]{2,1,0:T(8,128)} async-done(((f32[6,128,256]{2,1,0:T(8,128)}), f32[6,128,256]{2,1,0:T(8,128)}) %all-reduce.2.cloned.1.call-update) | async-done | bytes 786448 | tf_op jit(solution)/shard_map/psum | solution.py:34
  108.5 2.2 %and_select_fusion.1 = f32[6,128,256]{2,1,0:T(8,128)} fusion(f32[6,128,256]{2,1,0:T(8,128)} %all-reduce.2.cloned.1.call-done, pred[6,256]{1,0:T(8,128)(4,1)S(1)} %get-tuple-element.28, pred[6,128]{1,0:T(8,128)(4,1)S(1)} %broadcast_compare_fusion), kind=kLoop, calls=%fused_computation.36 | loop fusion | flops 393216 | bytes 1575168 | tf_op jit(solution)/shard_map/jit(_where)/select_n | solution.py:36
  (14 shorter events, 0.1 us)
Async XLA Ops:
  6.5 48.9 %copy-start = (bf16[3,6,256,256]{3,2,1,0:T(8,128)(2,1)S(1)}, bf16[3,6,256,256]{3,2,1,0:T(8,128)(2,1)}, u32[]{:S(2)}) copy-start(bf16[3,6,256,256]{3,2,1,0:T(8,128)(2,1)} %param.11) | copy-start | bytes 7077892
  11.8 8.8 %copy-start.1 = (s32[6,3,4]{0,2,1:T(4,128)S(1)}, s32[6,3,4]{0,2,1:T(4,128)}, u32[]{:S(2)}) copy-start(s32[6,3,4]{0,2,1:T(4,128)} %param.13) | copy-start | bytes 868
  11.8 9.1 %copy-start.2 = (f32[6,3,4]{0,2,1:T(4,128)S(1)}, f32[6,3,4]{0,2,1:T(4,128)}, u32[]{:S(2)}) copy-start(f32[6,3,4]{0,2,1:T(4,128)} %param.12) | copy-start | bytes 868
  14.2 32.0 %all-to-all-start = ((bf16[4,2,256,256]{3,2,1,0:T(8,128)(2,1)}), bf16[4,2,256,256]{3,2,1,0:T(8,128)(2,1)S(1)}, u32[]{:S(2)}, u32[]{:S(2)}) async-start(bf16[4,2,256,256]{3,2,1,0:T(8,128)(2,1)} %broadcast_select_fusion), calls=%async_computation | async-start | bytes 2097152 | tf_op jit(solution)/shard_map/all_to_all | solution.py:22
  20.5 87.9 %all-reduce.2.cloned.1.call-start = ((), (), s32[]{:S(2)}) async-start(), calls=%async_computation.1 | async-start | bytes 1572864 | tf_op jit(solution)/shard_map/psum | solution.py:34
Sparse Core Ops, SparseCore 0:
  75.0 33.4 all-reduce.1
where the time goes:
time: 118 us; the launch traced here: 117 us
  waiting for transfers between devices  57.6 us (49%)
  matrix products  16.7 us (14%)
  local copies, waits for them, and re-layouts  13.5 us (11%)
  between operations  13.5 us (11%)
  other arithmetic  9.91 us (8%)
  starting transfers between devices  6.32 us (5%)
    psum x1, waiting for transfers between devices, body(): summed = lax.psum(total, 'chan')  33.5 us
    all_to_all x1, waiting for transfers between devices, body(): lax.all_to_all(outgoing, 'sector', split_axis=0, concat_axis=0, tiled=True)  24.1 us
    dot_general x4, matrix products, body(): jnp.einsum('owhn,wopn->owhp', partial_left, right_env, preferred_element_...  16.7 us
    gather x4, local copies, waits for them, and re-layouts, body(): source = jnp.take(received, term_slot[:, :, position], axis=0)  9.2 us
    all_to_all x1, starting transfers between devices, body(): lax.all_to_all(outgoing, 'sector', split_axis=0, concat_axis=0, tiled=True)  6.32 us
    select_n x3, other arithmetic, body(): outgoing = jnp.take(masked, jnp.take(need, owner, axis=1), axis=0)  3.36 us
    add x1, other arithmetic, body(): total + jnp.sum(image * coef[:, :, position][:, :, None, None], axis=1)  2.69 us
  transfers between devices with their start and end apart: 2, of which 2 were waited for; matrix products, arithmetic and copies ran while one was open for 1% of the time, Pallas kernels for 0%

commit v1 on v0

v1 whole, which is shorter than its diff:
```python
import functools

import jax
import jax.numpy as jnp
from jax import lax
from jax.experimental import pallas as pl
from jax.experimental.pallas import tpu as pltpu
from jax.sharding import PartitionSpec as P

MESH = pl.DeviceIdType.MESH


def live(block, row_start, rows_live, cols_live):
    row = row_start + lax.broadcasted_iota(jnp.int32, block.shape, 0)
    col = lax.broadcasted_iota(jnp.int32, block.shape, 1)
    keep = jnp.logical_and(row < rows_live, col < cols_live)
    return jnp.where(keep, block, jnp.zeros_like(block))


def kernel(
    n_sector, n_chan, n_rep,
    coef, slots, need, dims, theta_hbm, left_hbm, right_hbm, out_hbm,
    theta, left, right, outgoing, source, totals, result,
    local_sem, out_sem, z_send, z_recv, x_send, x_recv, f_send, f_recv, y_send, y_recv,
):
    channels, blocks, half_rows, order = left.shape
    cap = need.shape[2]
    terms = slots.shape[2]
    me = lax.axis_index("sector")
    chan = lax.axis_index("chan")
    rep = lax.axis_index("rep")
    other = 1 - rep
    piece_rows = order // (n_chan * n_rep)

    theta_copy = pltpu.make_async_copy(theta_hbm, theta, local_sem.at[0])
    left_copy = pltpu.make_async_copy(left_hbm, left, local_sem.at[1])
    right_copy = pltpu.make_async_copy(right_hbm, right, local_sem.at[2])
    theta_copy.start()
    left_copy.start()
    right_copy.start()

    def each_sector(act):
        def step(i, carry):
            s = me + (1 - 2 * (i % 2)) * (i // 2 + 1)

            @pl.when(jnp.logical_and(s >= 0, s < n_sector))
            def _():
                act(s)

            return carry

        lax.fori_loop(0, 2 * (n_sector - 1), step, 0)

    def each_chan(act):
        def step(i, carry):
            act((chan + i) % n_chan)
            return carry

        lax.fori_loop(1, n_chan, step, 0)

    barrier = pltpu.get_barrier_semaphore()
    each_sector(lambda s: pl.semaphore_signal(barrier, 1, device_id={"sector": s}, device_id_type=MESH))
    each_chan(lambda c: pl.semaphore_signal(barrier, 1, device_id={"chan": c}, device_id_type=MESH))
    pl.semaphore_signal(barrier, 1, device_id={"rep": other}, device_id_type=MESH)

    def start_of(c, r):
        return pl.multiple_of((c * n_rep + r) * piece_rows, piece_rows)

    def piece(s, c, r):
        return source.at[pl.ds(s * cap, cap), pl.ds(start_of(c, r), piece_rows), :]

    def z_copy(s, at):
        return pltpu.make_async_remote_copy(
            src_ref=outgoing.at[s], dst_ref=piece(at, chan, rep),
            send_sem=z_send.at[s], recv_sem=z_recv.at[at],
            device_id={"sector": s}, device_id_type=MESH)

    def x_copy(s, c, at):
        return pltpu.make_async_remote_copy(
            src_ref=piece(s, chan, rep), dst_ref=piece(s, at, rep),
            send_sem=x_send.at[s, c], recv_sem=x_recv.at[s, at],
            device_id={"chan": c}, device_id_type=MESH)

    def f_copy(s, c, r):
        return pltpu.make_async_remote_copy(
            src_ref=piece(s, c, rep), dst_ref=piece(s, c, r),
            send_sem=f_send.at[s, c], recv_sem=f_recv.at[s, c],
            device_id={"rep": other}, device_id_type=MESH)

    def y_copy(o, c, at):
        return pltpu.make_async_remote_copy(
            src_ref=totals.at[chan, o], dst_ref=totals.at[at, o],
            send_sem=y_send.at[c, o], recv_sem=y_recv.at[at, o],
            device_id={"chan": c}, device_id_type=MESH)

    theta_copy.wait()
    pl.semaphore_wait(barrier, n_sector - 1 + n_chan - 1 + 1)

    def send_theta(s):
        for c in range(cap):
            b = need[s, me, c]
            first = start_of(chan, rep)
            rows = theta[b, pl.ds(first, piece_rows), :].astype(jnp.float32)
            outgoing[s, c] = live(rows, first, dims[b, 0], dims[b, 1]).astype(jnp.bfloat16)
        z_copy(s, me).start()

    each_sector(send_theta)

    for c in range(cap):
        b = need[me, me, c]
        whole = theta[b].astype(jnp.float32)
        source[me * cap + c] = live(whole, 0, dims[b, 0], dims[b, 1]).astype(jnp.bfloat16)

    def pass_on(s):
        z_copy(s, s).wait_recv()
        each_chan(lambda c: x_copy(s, c, chan).start())
        f_copy(s, chan, rep).start()

    each_sector(pass_on)

    def pass_second(s):
        def one(c):
            x_copy(s, c, c).wait_recv()
            f_copy(s, c, rep).start()

        each_chan(one)

    each_sector(pass_second)
    left_copy.wait()
    right_copy.wait()

    def gather_rest(s):
        f_copy(s, chan, other).wait_recv()
        each_chan(lambda c: f_copy(s, c, other).wait_recv())

    each_sector(gather_rest)

    def block_product(o, carry):
        total = jnp.zeros((half_rows, order), jnp.float32)
        for w in range(channels):
            mixed = jnp.zeros((half_rows, order), jnp.float32)
            for k in range(terms):
                partial = jnp.dot(
                    left[w, o], source[slots[o, w, k]], preferred_element_type=jnp.float32
                ).astype(jnp.bfloat16)
                mixed = mixed + coef[o, w, k] * partial.astype(jnp.float32)
            high = mixed.astype(jnp.bfloat16)
            low = (mixed - high.astype(jnp.float32)).astype(jnp.bfloat16)
            for part in (high, low):
                total = total + lax.dot_general(
                    part, right[w, o], (((1,), (1,)), ((), ())), preferred_element_type=jnp.float32
                )
        totals[chan, o] = total.astype(jnp.bfloat16)
        each_chan(lambda c: y_copy(o, c, chan).start())
        return carry

    lax.fori_loop(0, blocks, block_product, 0)

    def finish(o, carry):
        each_chan(lambda c: y_copy(o, c, c).wait_recv())
        total = totals[0, o].astype(jnp.float32)
        for c in range(1, n_chan):
            total = total + totals[c, o].astype(jnp.float32)
        result[o] = live(total, rep * half_rows, dims[o, 0], dims[o, 1])
        pltpu.make_async_copy(result.at[o], out_hbm.at[o], out_sem.at[o]).start()
        return carry

    lax.fori_loop(0, blocks, finish, 0)

    def drain_theta(s):
        z_copy(s, me).wait_send()
        each_chan(lambda c: x_copy(s, c, chan).wait_send())
        f_copy(s, chan, rep).wait_send()
        each_chan(lambda c: f_copy(s, c, rep).wait_send())

    each_sector(drain_theta)

    def drain(o, carry):
        each_chan(lambda c: y_copy(o, c, chan).wait_send())
        pltpu.make_async_copy(result.at[o], out_hbm.at[o], out_sem.at[o]).wait()
        return carry

    lax.fori_loop(0, blocks, drain, 0)


def body(n_sector, n_chan, n_rep, theta, left_env, right_env, coef, term_slot, need, dims):
    blocks, order, _ = theta.shape
    channels, _, half_rows, _ = left_env.shape
    cap = need.shape[2]
    dma = pltpu.SemaphoreType.DMA
    smem = pl.BlockSpec(memory_space=pltpu.SMEM)
    hbm = pl.BlockSpec(memory_space=pl.ANY)
    flops = 2 * blocks * channels * (term_slot.shape[2] + 2) * half_rows * order * order
    return pl.pallas_call(
        functools.partial(kernel, n_sector, n_chan, n_rep),
        out_shape=jax.ShapeDtypeStruct((blocks, half_rows, order), jnp.float32),
        in_specs=[smem] * 4 + [hbm] * 3,
        out_specs=hbm,
        scratch_shapes=[
            pltpu.VMEM(theta.shape, jnp.bfloat16),
            pltpu.VMEM(left_env.shape, jnp.bfloat16),
            pltpu.VMEM(right_env.shape, jnp.bfloat16),
            pltpu.VMEM((n_sector, cap, order // (n_chan * n_rep), order), jnp.bfloat16),
            pltpu.VMEM((n_sector * cap, order, order), jnp.bfloat16),
            pltpu.VMEM((n_chan, blocks, half_rows, order), jnp.bfloat16),
            pltpu.VMEM((blocks, half_rows, order), jnp.float32),
            dma((3,)),
            dma((blocks,)),
            dma((n_sector,)),
            dma((n_sector,)),
            dma((n_sector, n_chan)),
            dma((n_sector, n_chan)),
            dma((n_sector, n_chan)),
            dma((n_sector, n_chan)),
            dma((n_chan, blocks)),
            dma((n_chan, blocks)),
        ],
        compiler_params=pltpu.CompilerParams(
            collective_id=0, has_side_effects=True, vmem_limit_bytes=40 * 1024 * 1024
        ),
        cost_estimate=pl.CostEstimate(flops=flops, bytes_accessed=6 * 1024 * 1024, transcendentals=0),
        name="product",
    )(coef, term_slot, need, dims, theta, left_env, right_env)


def solution(mesh):
    in_specs = (
        P(("groups", "sector"), None, None),
        P(("groups", "chan"), "sector", "rep", None),
        P(("groups", "chan"), "sector", None, None),
        P(("groups", "sector"), "chan", None),
        P(("groups", "sector"), "chan", None),
        P("groups", None, None),
        P(("groups", "sector"), None),
    )
    out_specs = P(("groups", "sector"), "rep", None)
    sizes = mesh.shape
    local = functools.partial(body, sizes["sector"], sizes["chan"], sizes["rep"])
    return jax.shard_map(local, mesh=mesh, in_specs=in_specs, out_specs=out_specs, check_vma=False)
```

time: 118 us -> 38.1 us (0.32)
  waiting for transfers between devices: 57.6 us -> 0 us
  Pallas kernels: 0 us -> 29.7 us
  matrix products: 16.7 us -> 0 us
  between operations: 13.5 us -> 0.01 us
  other arithmetic: 9.91 us -> 0 us
  starting transfers between devices: 6.32 us -> 0 us
  local copies, waits for them, and re-layouts: 13.5 us -> 8.09 us
    psum x1 -> x0, waiting for transfers between devices: 33.5 us -> none  [body(): summed = lax.psum(total, 'chan')]
    pallas_call x0 -> x1, Pallas kernels: none -> 29.7 us  [body(): pl.pallas_call(functools.partial(kernel, n_sector, n_chan, n_rep), out_sh...]
    all_to_all x1 -> x0, waiting for transfers between devices: 24.1 us -> none  [body(): lax.all_to_all(outgoing, 'sector', split_axis=0, concat_axis=0, tiled=True)]
    dot_general x4 -> x0, matrix products: 16.7 us -> none  [body(): jnp.einsum('owhn,wopn->owhp', partial_left, right_env, preferred_element_...]
    gather x5 -> x0, local copies, waits for them, and re-layouts: 10.8 us -> none  [the longest x4 9.2 us: body(): source = jnp.take(received, term_slot[:, :, position], axis=0)]
    unnamed x6 -> x11, local copies, waits for them, and re-layouts: 0.01 us -> 8.09 us
    select_n x7 -> x0, other arithmetic: 7.01 us -> none  [the longest x3 3.36 us: body(): outgoing = jnp.take(masked, jnp.take(need, owner, axis=1), axis=0)]
    all_to_all x1 -> x0, starting transfers between devices: 6.32 us -> none  [body(): lax.all_to_all(outgoing, 'sector', split_axis=0, concat_axis=0, tiled=True)]
  transfers between devices with their start and end apart: 2 -> 0, of which waited for: 2 -> 0; matrix products, arithmetic and copies ran while one was open for 1% -> 0% of each run, Pallas kernels for 0% -> 0%
where the time goes in v1:
time: 38.1 us; the launch traced here: 37.8 us
  Pallas kernels  29.7 us (78%)
  local copies, waits for them, and re-layouts  8.09 us (21%)
    pallas_call x1, Pallas kernels, body(): pl.pallas_call(functools.partial(kernel, n_sector, n_chan, n_rep), out_sh...  29.7 us
    unnamed x11, local copies, waits for them, and re-layouts  8.09 us

profile of v1, /device:TPU:0, one launch (start us, length us, event | category | flops | bytes accessed | tf_op | source)
XLA Modules:
  0.0 37.8 jit_solution(15075291106431299320)
XLA Ops:
  0.0 0.8 %copy.11.dims = s32[6,2]{1,0:T(8,128)S(1)} copy(s32[6,2]{0,1:T(2,128)} %param.13) | data formatting | bytes 96 | tf_op args[6]
  0.8 0.8 %copy.10.need = s32[4,4,2]{2,1,0:T(4,128)S(1)} copy(s32[4,4,2]{1,2,0:T(2,128)} %param.12) | data formatting | bytes 256 | tf_op args[5]
  1.6 0.8 %copy.8.coef = f32[6,3,4]{2,1,0:T(4,128)S(1)} copy(f32[6,3,4]{0,2,1:T(4,128)} %param.10) | data formatting | bytes 576 | tf_op args[3]
  2.3 0.8 %copy.9.slots = s32[6,3,4]{2,1,0:T(4,128)S(1)} copy(s32[6,3,4]{0,2,1:T(4,128)} %param.11) | data formatting | bytes 576 | tf_op args[4]
  3.1 0.0 copy-start
  3.1 1.7 %copy-done = bf16[3,6,256,256]{3,2,1,0:T(8,128)(2,1)S(1)} copy-done((bf16[3,6,256,256]{3,2,1,0:T(8,128)(2,1)S(1)}, bf16[3,6,256,256]{3,2,1,0:T(8,128)(2,1)}, u32[]{:S(2)}) %copy-start) | copy-done | bytes 2359320
  4.8 0.0 copy-start.1
  4.8 1.3 %copy-done.1 = bf16[3,6,128,256]{3,2,1,0:T(8,128)(2,1)S(1)} copy-done((bf16[3,6,128,256]{3,2,1,0:T(8,128)(2,1)S(1)}, bf16[3,6,128,256]{3,2,1,0:T(8,128)(2,1)}, u32[]{:S(2)}) %copy-start.1) | copy-done | bytes 1179672
  6.1 0.0 copy-start.2
  6.1 1.1 %copy-done.2 = bf16[6,256,256]{2,1,0:T(8,128)(2,1)S(1)} copy-done((bf16[6,256,256]{2,1,0:T(8,128)(2,1)S(1)}, bf16[6,256,256]{2,1,0:T(8,128)(2,1)}, u32[]{:S(2)}) %copy-start.2) | copy-done | bytes 786456
  7.2 29.7 %product.1 = f32[6,128,256]{2,1,0:T(8,128)S(1)} custom-call(f32[6,3,4]{2,1,0:T(4,128)S(1)} %copy.8.coef, s32[6,3,4]{2,1,0:T(4,128)S(1)} %copy.9.slots, s32[4,4,2]{2,1,0:T(4,128)S(1)} %copy.10.need, s32[6,2]{1,0:T(8,128)S(1)} %copy.11.dims, bf16[6,256,256]{2,1,0:T(8,128)(2,1)S(1)} %copy-done.2, bf16[3,6,128,256]{3,2,1,0:T(8,128)(2,1)S(1)} %copy-done.1, ...), custom_call_target="tpu_custom_call" | custom-call | flops 1811939328 | bytes 6291456 | tf_op jit(solution)/shard_map/product/pallas_call | solution.py:194
  36.9 0.9 %copy.13 = f32[6,128,256]{2,1,0:T(8,128)} copy(f32[6,128,256]{2,1,0:T(8,128)S(1)} %product.1) | data formatting | bytes 1572864
Async XLA Ops:
  3.1 1.7 %copy-start = (bf16[3,6,256,256]{3,2,1,0:T(8,128)(2,1)S(1)}, bf16[3,6,256,256]{3,2,1,0:T(8,128)(2,1)}, u32[]{:S(2)}) copy-start(bf16[3,6,256,256]{3,2,1,0:T(8,128)(2,1)} %right_hbm.1) | copy-start | bytes 7077892
  4.8 1.3 %copy-start.1 = (bf16[3,6,128,256]{3,2,1,0:T(8,128)(2,1)S(1)}, bf16[3,6,128,256]{3,2,1,0:T(8,128)(2,1)}, u32[]{:S(2)}) copy-start(bf16[3,6,128,256]{3,2,1,0:T(8,128)(2,1)} %left_hbm.1) | copy-start | bytes 3538948
  6.1 1.1 %copy-start.2 = (bf16[6,256,256]{2,1,0:T(8,128)(2,1)S(1)}, bf16[6,256,256]{2,1,0:T(8,128)(2,1)}, u32[]{:S(2)}) copy-start(bf16[6,256,256]{2,1,0:T(8,128)(2,1)} %theta_hbm.1) | copy-start | bytes 2359300

commit v2 on v1

v2 whole, which is shorter than its diff:
```python
import functools

import jax
import jax.numpy as jnp
from jax import lax
from jax.experimental import pallas as pl
from jax.experimental.pallas import tpu as pltpu
from jax.sharding import PartitionSpec as P

MESH = pl.DeviceIdType.MESH


def live(block, row_start, rows_live, cols_live):
    row = row_start + lax.broadcasted_iota(jnp.int32, block.shape, 0)
    col = lax.broadcasted_iota(jnp.int32, block.shape, 1)
    keep = jnp.logical_and(row < rows_live, col < cols_live)
    return jnp.where(keep, block, jnp.zeros_like(block))


def shared_rows(half_rows, n_chan):
    return 16 * max(1, half_rows // (2 * 16 * n_chan))


def kernel(
    n_sector, n_chan, n_rep,
    coef, slots, need, dims, theta_hbm, left_hbm, right_hbm, out_hbm,
    theta, left, right, outgoing, source, totals,
    local_sem, out_sem, z_send, z_recv, x_send, x_recv, d_send, d_recv, f_send, f_recv, y_send, y_recv,
):
    channels, blocks, half_rows, order = left.shape
    cap = need.shape[1]
    terms = slots.shape[1]
    me = lax.axis_index("sector")
    chan = lax.axis_index("chan")
    rep = lax.axis_index("rep")
    other = 1 - rep
    piece_rows = shared_rows(half_rows, n_chan)
    direct_rows = half_rows - piece_rows * n_chan

    theta_copy = pltpu.make_async_copy(theta_hbm, theta, local_sem.at[0])
    left_copy = pltpu.make_async_copy(left_hbm, left, local_sem.at[1])
    right_copy = pltpu.make_async_copy(right_hbm, right, local_sem.at[2])
    theta_copy.start()
    left_copy.start()
    right_copy.start()

    def each_sector(act):
        for d in range(1, n_sector):
            act((me + d) % n_sector)

    def each_chan(act):
        for d in range(1, n_chan):
            act((chan + d) % n_chan)

    barrier = pltpu.get_barrier_semaphore()
    each_sector(lambda s: pl.semaphore_signal(barrier, 1, device_id={"sector": s}, device_id_type=MESH))
    each_chan(lambda c: pl.semaphore_signal(barrier, 1, device_id={"chan": c}, device_id_type=MESH))
    pl.semaphore_signal(barrier, 1, device_id={"rep": other}, device_id_type=MESH)

    def start_of(c, r):
        return pl.multiple_of(r * half_rows + c * piece_rows, 16)

    def piece(s, c, r):
        rows = direct_rows if isinstance(c, int) and c == n_chan else piece_rows
        return source.at[pl.ds(s * cap, cap), pl.ds(start_of(c, r), rows), :]

    def z_copy(s, at):
        return pltpu.make_async_remote_copy(
            src_ref=outgoing.at[s, :, pl.ds(0, piece_rows), :], dst_ref=piece(at, chan, rep),
            send_sem=z_send.at[s], recv_sem=z_recv.at[at],
            device_id={"sector": s}, device_id_type=MESH)

    def d_copy(s, at):
        return pltpu.make_async_remote_copy(
            src_ref=outgoing.at[s, :, pl.ds(piece_rows, direct_rows), :], dst_ref=piece(at, n_chan, rep),
            send_sem=d_send.at[s], recv_sem=d_recv.at[at],
            device_id={"sector": s}, device_id_type=MESH)

    def x_copy(s, c, at):
        return pltpu.make_async_remote_copy(
            src_ref=piece(s, chan, rep), dst_ref=piece(s, at, rep),
            send_sem=x_send.at[s, c], recv_sem=x_recv.at[s, at],
            device_id={"chan": c}, device_id_type=MESH)

    def f_copy(s, c, r):
        return pltpu.make_async_remote_copy(
            src_ref=piece(s, c, rep), dst_ref=piece(s, c, r),
            send_sem=f_send.at[s, c], recv_sem=f_recv.at[s, c],
            device_id={"rep": other}, device_id_type=MESH)

    def y_copy(o, c, at):
        return pltpu.make_async_remote_copy(
            src_ref=totals.at[o], dst_ref=out_hbm.at[at, o],
            send_sem=y_send.at[c, o], recv_sem=y_recv.at[at, o],
            device_id={"chan": c}, device_id_type=MESH)

    theta_copy.wait()
    def prepare(s):
        for k in range(cap):
            b = need[s, k, me]
            for c, at, rows in ((chan, 0, piece_rows), (n_chan, piece_rows, direct_rows)):
                if rows:
                    first = start_of(c, rep)
                    part = theta[b, pl.ds(first, rows), :].astype(jnp.float32)
                    part = live(part, first, dims[0, b], dims[1, b]).astype(jnp.bfloat16)
                    outgoing[s, k, pl.ds(at, rows), :] = part

    each_sector(prepare)
    for c in range(cap):
        b = need[me, c, me]
        whole = theta[b].astype(jnp.float32)
        source[me * cap + c] = live(whole, 0, dims[0, b], dims[1, b]).astype(jnp.bfloat16)

    pl.semaphore_wait(barrier, n_sector - 1 + n_chan - 1 + 1)

    each_sector(lambda s: z_copy(s, me).start())

    def pass_on(s):
        z_copy(s, s).wait_recv()
        each_chan(lambda c: x_copy(s, c, chan).start())
        f_copy(s, chan, rep).start()

    if direct_rows:
        each_sector(lambda s: d_copy(s, me).start())
    each_sector(pass_on)

    def pass_second(s):
        def one(c):
            x_copy(s, c, c).wait_recv()
            f_copy(s, c, rep).start()

        each_chan(one)

    each_sector(pass_second)

    def pass_direct(s):
        d_copy(s, s).wait_recv()
        f_copy(s, n_chan, rep).start()

    if direct_rows:
        each_sector(pass_direct)
    left_copy.wait()
    right_copy.wait()

    def gather_rest(s):
        f_copy(s, chan, other).wait_recv()
        each_chan(lambda c: f_copy(s, c, other).wait_recv())
        if direct_rows:
            f_copy(s, n_chan, other).wait_recv()

    each_sector(gather_rest)

    def own_copy(o):
        return pltpu.make_async_copy(totals.at[o], out_hbm.at[chan, o], out_sem.at[o])

    def block_product(o, carry):
        total = jnp.zeros((half_rows, order), jnp.float32)
        for w in range(channels):
            mixed = jnp.zeros((half_rows, order), jnp.float32)
            for k in range(terms):
                partial = jnp.dot(
                    left[w, o], source[slots[w, k, o]], preferred_element_type=jnp.float32
                ).astype(jnp.bfloat16)
                mixed = mixed + coef[w, k, o] * partial.astype(jnp.float32)
            high = mixed.astype(jnp.bfloat16)
            low = (mixed - high.astype(jnp.float32)).astype(jnp.bfloat16)
            for part in (high, low):
                total = total + lax.dot_general(
                    part, right[w, o], (((1,), (1,)), ((), ())), preferred_element_type=jnp.float32
                )
        totals[o] = live(total, rep * half_rows, dims[0, o], dims[1, o]).astype(jnp.bfloat16)
        each_chan(lambda c: y_copy(o, c, chan).start())
        own_copy(o).start()
        return carry

    lax.fori_loop(0, blocks, block_product, 0)

    def finish(o, carry):
        each_chan(lambda c: y_copy(o, c, c).wait_recv())
        return carry

    lax.fori_loop(0, blocks, finish, 0)

    def drain_theta(s):
        z_copy(s, me).wait_send()
        each_chan(lambda c: x_copy(s, c, chan).wait_send())
        f_copy(s, chan, rep).wait_send()
        each_chan(lambda c: f_copy(s, c, rep).wait_send())
        if direct_rows:
            d_copy(s, me).wait_send()
            f_copy(s, n_chan, rep).wait_send()

    each_sector(drain_theta)

    def drain(o, carry):
        each_chan(lambda c: y_copy(o, c, chan).wait_send())
        own_copy(o).wait()
        return carry

    lax.fori_loop(0, blocks, drain, 0)


def body(n_sector, n_chan, n_rep, theta, left_env, right_env, coef, term_slot, need, dims):
    blocks, order, _ = theta.shape
    channels, _, half_rows, _ = left_env.shape
    cap = need.shape[2]
    dma = pltpu.SemaphoreType.DMA
    rows_out = half_rows - (n_chan - 1) * shared_rows(half_rows, n_chan)
    smem = pl.BlockSpec(memory_space=pltpu.SMEM)
    hbm = pl.BlockSpec(memory_space=pl.ANY)
    flops = 2 * blocks * channels * (term_slot.shape[2] + 2) * half_rows * order * order
    totals = pl.pallas_call(
        functools.partial(kernel, n_sector, n_chan, n_rep),
        out_shape=jax.ShapeDtypeStruct((n_chan, blocks, half_rows, order), jnp.bfloat16),
        in_specs=[smem] * 4 + [hbm] * 3,
        out_specs=hbm,
        scratch_shapes=[
            pltpu.VMEM(theta.shape, jnp.bfloat16),
            pltpu.VMEM(left_env.shape, jnp.bfloat16),
            pltpu.VMEM(right_env.shape, jnp.bfloat16),
            pltpu.VMEM((n_sector, cap, rows_out, order), jnp.bfloat16),
            pltpu.VMEM((n_sector * cap, order, order), jnp.bfloat16),
            pltpu.VMEM((blocks, half_rows, order), jnp.bfloat16),
            dma((3,)),
            dma((blocks,)),
            dma((n_sector,)),
            dma((n_sector,)),
            dma((n_sector, n_chan)),
            dma((n_sector, n_chan)),
            dma((n_sector,)),
            dma((n_sector,)),
            dma((n_sector, n_chan + 1)),
            dma((n_sector, n_chan + 1)),
            dma((n_chan, blocks)),
            dma((n_chan, blocks)),
        ],
        compiler_params=pltpu.CompilerParams(
            collective_id=0, has_side_effects=True, vmem_limit_bytes=60 * 1024 * 1024
        ),
        cost_estimate=pl.CostEstimate(flops=flops, bytes_accessed=6 * 1024 * 1024, transcendentals=0),
        name="product",
    )(
        coef.transpose(1, 2, 0), term_slot.transpose(1, 2, 0), need.transpose(0, 2, 1), dims.T,
        theta, left_env, right_env,
    )
    total = totals[0].astype(jnp.float32)
    for c in range(1, n_chan):
        total = total + totals[c].astype(jnp.float32)
    return total


def solution(mesh):
    in_specs = (
        P(("groups", "sector"), None, None),
        P(("groups", "chan"), "sector", "rep", None),
        P(("groups", "chan"), "sector", None, None),
        P(("groups", "sector"), "chan", None),
        P(("groups", "sector"), "chan", None),
        P("groups", None, None),
        P(("groups", "sector"), None),
    )
    out_specs = P(("groups", "sector"), "rep", None)
    sizes = mesh.shape
    local = functools.partial(body, sizes["sector"], sizes["chan"], sizes["rep"])
    return jax.shard_map(local, mesh=mesh, in_specs=in_specs, out_specs=out_specs, check_vma=False)
```

time: 38.1 us -> 30 us (0.79)
  local copies, waits for them, and re-layouts: 8.09 us -> 0 us
  Pallas kernels: 29.7 us -> 27.6 us
  other arithmetic: 0 us -> 2.08 us
    unnamed x11 -> x0, local copies, waits for them, and re-layouts: 8.09 us -> none
    pallas_call x1, Pallas kernels: 29.7 us -> 27.6 us  [body(): pl.pallas_call(functools.partial(kernel, n_sector, n_chan, n_rep), out_sh...]
    add x0 -> x1, other arithmetic: none -> 2.08 us  [body(): total = total + totals[c].astype(jnp.float32)]
where the time goes in v2:
time: 30 us; the launch traced here: 29.6 us
  Pallas kernels  27.6 us (92%)
  other arithmetic  2.08 us (7%)
    pallas_call x1, Pallas kernels, body(): pl.pallas_call(functools.partial(kernel, n_sector, n_chan, n_rep), out_sh...  27.6 us
    add x1, other arithmetic, body(): total = total + totals[c].astype(jnp.float32)  2.08 us

profile of v2, /device:TPU:0, one launch (start us, length us, event | category | flops | bytes accessed | tf_op | source)
XLA Modules:
  0.0 29.6 jit_solution(12819609795236099287)
XLA Ops:
  0.0 27.6 %product.1 = bf16[2,6,128,256]{3,2,1,0:T(8,128)(2,1)} custom-call(f32[3,4,6]{2,1,0:T(4,128)} %bitcast.6, s32[3,4,6]{2,1,0:T(4,128)} %bitcast.7, s32[4,2,4]{2,1,0:T(2,128)} %bitcast.8, s32[2,6]{1,0:T(2,128)} %bitcast.9, bf16[6,256,256]{2,1,0:T(8,128)(2,1)} %theta_hbm.1, bf16[3,6,128,256]{3,2,1,0:T(8,128)(2,1)} %left_hbm.1, bf16[3,6,256,256]{3,2,1,0:T(8,128)(2,1)} %right_hbm.1), custom_call_target="tpu_custom_call" | custom-call | flops 1811939328 | bytes 6291456 | tf_op jit(solution)/shard_map/product/pallas_call | solution.py:212
  27.6 2.1 %add_bitcast_fusion = f32[6,128,256]{2,1,0:T(8,128)} fusion(bf16[2,6,128,256]{3,2,1,0:T(8,128)(2,1)} %product.1), kind=kLoop, calls=%fused_computation | loop fusion | flops 589824 | bytes 1572864 | tf_op jit(solution)/shard_map/add | solution.py:248

commit v3 on v2

--- a/solution.py
+++ b/solution.py
@@ -164,10 +164,11 @@
                 mixed = mixed + coef[w, k, o] * partial.astype(jnp.float32)
             high = mixed.astype(jnp.bfloat16)
             low = (mixed - high.astype(jnp.float32)).astype(jnp.bfloat16)
-            for part in (high, low):
-                total = total + lax.dot_general(
-                    part, right[w, o], (((1,), (1,)), ((), ())), preferred_element_type=jnp.float32
-                )
+            image = lax.dot_general(
+                jnp.concatenate([high, low], axis=0), right[w, o],
+                (((1,), (1,)), ((), ())), preferred_element_type=jnp.float32,
+            )
+            total = total + (image[:half_rows] + image[half_rows:])
         totals[o] = live(total, rep * half_rows, dims[0, o], dims[1, o]).astype(jnp.bfloat16)
         each_chan(lambda c: y_copy(o, c, chan).start())
         own_copy(o).start()

time: 30 us -> 29.8 us (level)
  Pallas kernels: 27.6 us -> 27.2 us
    pallas_call x1, Pallas kernels: 27.6 us -> 27.2 us  [body(): pl.pallas_call(functools.partial(kernel, n_sector, n_chan, n_rep), out_sh...]
where the time goes in v3:
time: 29.8 us; the launch traced here: 29.3 us
  Pallas kernels  27.2 us (91%)
  other arithmetic  2.08 us (7%)
    pallas_call x1, Pallas kernels, body(): pl.pallas_call(functools.partial(kernel, n_sector, n_chan, n_rep), out_sh...  27.2 us
    add x1, other arithmetic, body(): total = total + totals[c].astype(jnp.float32)  2.08 us

profile of v3, /device:TPU:0, one launch (start us, length us, event | category | flops | bytes accessed | tf_op | source)
XLA Modules:
  0.0 29.3 jit_solution(8416214337170269099)
XLA Ops:
  0.0 27.2 %product.1 = bf16[2,6,128,256]{3,2,1,0:T(8,128)(2,1)} custom-call(f32[3,4,6]{2,1,0:T(4,128)} %bitcast.6, s32[3,4,6]{2,1,0:T(4,128)} %bitcast.7, s32[4,2,4]{2,1,0:T(2,128)} %bitcast.8, s32[2,6]{1,0:T(2,128)} %bitcast.9, bf16[6,256,256]{2,1,0:T(8,128)(2,1)} %theta_hbm.1, bf16[3,6,128,256]{3,2,1,0:T(8,128)(2,1)} %left_hbm.1, bf16[3,6,256,256]{3,2,1,0:T(8,128)(2,1)} %right_hbm.1), custom_call_target="tpu_custom_call" | custom-call | flops 1811939328 | bytes 6291456 | tf_op jit(solution)/shard_map/product/pallas_call | solution.py:213
  27.2 2.1 %add_bitcast_fusion = f32[6,128,256]{2,1,0:T(8,128)} fusion(bf16[2,6,128,256]{3,2,1,0:T(8,128)(2,1)} %product.1), kind=kLoop, calls=%fused_computation | loop fusion | flops 589824 | bytes 1572864 | tf_op jit(solution)/shard_map/add | solution.py:249

commit v4 on v3

--- a/solution.py
+++ b/solution.py
@@ -19,6 +19,13 @@
 
 def shared_rows(half_rows, n_chan):
     return 16 * max(1, half_rows // (2 * 16 * n_chan))
+
+
+def add_shards(totals, out):
+    total = totals[0].astype(jnp.float32)
+    for c in range(1, totals.shape[0]):
+        total = total + totals[c].astype(jnp.float32)
+    out[...] = total
 
 
 def kernel(
@@ -244,10 +251,15 @@
         coef.transpose(1, 2, 0), term_slot.transpose(1, 2, 0), need.transpose(0, 2, 1), dims.T,
         theta, left_env, right_env,
     )
-    total = totals[0].astype(jnp.float32)
-    for c in range(1, n_chan):
-        total = total + totals[c].astype(jnp.float32)
-    return total
+    step = blocks // 2 if blocks % 2 == 0 else 1
+    return pl.pallas_call(
+        add_shards,
+        out_shape=jax.ShapeDtypeStruct((blocks, half_rows, order), jnp.float32),
+        grid=(blocks // step,),
+        in_specs=[pl.BlockSpec((n_chan, step, half_rows, order), lambda i: (0, i, 0, 0))],
+        out_specs=pl.BlockSpec((step, half_rows, order), lambda i: (i, 0, 0)),
+        name="add_shards",
+    )(totals)
 
 
 def solution(mesh):

time: 29.8 us -> 29.6 us (level)
  other arithmetic: 2.08 us -> 0 us
  Pallas kernels: 27.2 us -> 29.1 us
    add x1 -> x0, other arithmetic: 2.08 us -> none  [body(): total = total + totals[c].astype(jnp.float32)]
    pallas_call x0 -> x1, Pallas kernels: none -> 1.93 us  [body(): pl.pallas_call(add_shards, out_shape=jax.ShapeDtypeStruct((blocks, half_r...]
where the time goes in v4:
time: 29.6 us; the launch traced here: 29.1 us
  Pallas kernels  29.1 us (98%)
    pallas_call x1, Pallas kernels, body(): pl.pallas_call(functools.partial(kernel, n_sector, n_chan, n_rep), out_sh...  27.2 us
    pallas_call x1, Pallas kernels, body(): pl.pallas_call(add_shards, out_shape=jax.ShapeDtypeStruct((blocks, half_r...  1.93 us

profile of v4, /device:TPU:0, one launch (start us, length us, event | category | flops | bytes accessed | tf_op | source)
XLA Modules:
  0.0 29.1 jit_solution(17022407912606405148)
XLA Ops:
  0.0 27.2 %product.1.totals = bf16[2,6,128,256]{3,2,1,0:T(8,128)(2,1)} custom-call(f32[3,4,6]{2,1,0:T(4,128)} %bitcast.4, s32[3,4,6]{2,1,0:T(4,128)} %bitcast.5, s32[4,2,4]{2,1,0:T(2,128)} %bitcast.6, s32[2,6]{1,0:T(2,128)} %bitcast.7, bf16[6,256,256]{2,1,0:T(8,128)(2,1)} %theta_hbm.1, bf16[3,6,128,256]{3,2,1,0:T(8,128)(2,1)} %left_hbm.1, ...), custom_call_target="tpu_custom_call" | custom-call | flops 1811939328 | bytes 6291456 | tf_op jit(solution)/shard_map/product/pallas_call | solution.py:220
  27.2 1.9 %add_shards.1 = f32[6,128,256]{2,1,0:T(8,128)} custom-call(bf16[2,6,128,256]{3,2,1,0:T(8,128)(2,1)} %product.1.totals), custom_call_target="tpu_custom_call" | custom-call | tf_op jit(solution)/shard_map/add_shards/pallas_call | solution.py:255
